TPU v7x, 32 devices: a whole 2x2x4 slice. The times are simulated.
32 devices in a mesh: batch: 4 (over z), lon: 8 (over y, x, core).
Axes of the slice: x: 2, y: 2, z: 4, core: 2. Of those that a mesh axis runs over, the one named last changes fastest.
Arguments:
- fields: bfloat16 [8, 48, 64, 64], P('batch', None, 'lon'), may hold values from -6 to 6
- variable_ids: int32 [8, 48], P('batch'), may hold values from 0 to 47, each once within a row
- variable_mask: int32 [8, 48], P('batch'), may hold values from 0 to 1, as said below
- position: bfloat16 [32, 32, 1024], P('lon'), may hold values from -3 to 3
- patching: bfloat16 [1024, 192], replicated, may hold values from -3 to 3
- tagging: bfloat16 [1024, 48], replicated, may hold values from -6 to 6
- beacon: bfloat16 [1024], replicated, may hold values from -6 to 6
- keying: bfloat16 [1024, 1024], replicated, may hold values from -0.1875 to 0.1875
- valuing: bfloat16 [1024, 1024], replicated, may hold values from -0.1875 to 0.1875
- lifting: bfloat16 [1024], replicated, may hold values from -1.75 to 1.75
- merging: bfloat16 [1024, 1024], replicated, may hold values from -0.5 to 0.5
- offset: bfloat16 [1024], replicated, may hold values from -1.75 to 1.75
- scaling: bfloat16 [1024], replicated, may hold values from 0.25 to 1.75
- centre: bfloat16 [1024], replicated, may hold values from -1.75 to 1.75
- projecting: bfloat16 [1024, 3072], replicated, may hold values from -0.1875 to 0.1875
- biasing: bfloat16 [2048], replicated, may hold values from -1.75 to 1.75
- mixing: bfloat16 [1024, 1024], replicated, may hold values from -4 to 4
- nudging: bfloat16 [1024], replicated, may hold values from -1.75 to 1.75
- rescaling: bfloat16 [1024], replicated, may hold values from 0.25 to 1.75
- recentre: bfloat16 [1024], replicated, may hold values from -1.75 to 1.75
- widening: bfloat16 [1024, 4096], replicated, may hold values from -0.1875 to 0.1875
- uplift: bfloat16 [4096], replicated, may hold values from -1.75 to 1.75
- narrowing: bfloat16 [4096, 1024], replicated, may hold values from -0.09375 to 0.09375
- settle: bfloat16 [1024], replicated, may hold values from -1.75 to 1.75
- reading: bfloat16 [1024, 192], replicated, may hold values from -0.1875 to 0.1875
- baseline: bfloat16 [192], replicated, may hold values from -3 to 3
- cotangent: bfloat16 [8, 48, 64, 64], P('batch', None, 'lon'), may hold values from -6 to 6
Outputs:
- prediction: bfloat16 [8, 48, 64, 64], P('batch', None, 'lon')
- fields_gradient: float32 [8, 48, 64, 64], P('batch', None, 'lon')
- position_gradient: float32 [32, 32, 1024], P('lon')
- patching_gradient: float32 [1024, 192], P(('batch', 'lon'))
- tagging_gradient: float32 [1024, 48], P(('batch', 'lon'))
- beacon_gradient: float32 [1024], P(('batch', 'lon'))
- keying_gradient: float32 [1024, 1024], P(('batch', 'lon'))
- valuing_gradient: float32 [1024, 1024], P(('batch', 'lon'))
- lifting_gradient: float32 [1024], P(('batch', 'lon'))
- merging_gradient: float32 [1024, 1024], P(('batch', 'lon'))
- offset_gradient: float32 [1024], P(('batch', 'lon'))
- scaling_gradient: float32 [1024], P(('batch', 'lon'))
- centre_gradient: float32 [1024], P(('batch', 'lon'))
- projecting_gradient: float32 [1024, 3072], P(('batch', 'lon'))
- biasing_gradient: float32 [2048], P(('batch', 'lon'))
- mixing_gradient: float32 [1024, 1024], P(('batch', 'lon'))
- nudging_gradient: float32 [1024], P(('batch', 'lon'))
- rescaling_gradient: float32 [1024], P(('batch', 'lon'))
- recentre_gradient: float32 [1024], P(('batch', 'lon'))
- widening_gradient: float32 [1024, 4096], P(('batch', 'lon'))
- uplift_gradient: float32 [4096], P(('batch', 'lon'))
- narrowing_gradient: float32 [4096, 1024], P(('batch', 'lon'))
- settle_gradient: float32 [1024], P(('batch', 'lon'))
- reading_gradient: float32 [1024, 192], P(('batch', 'lon'))
- baseline_gradient: float32 [192], replicated
Inputs may be any that keep to these rules, and one draw needn't show every extreme that they name: `variable_mask`: each item keeps between 30 and 48 of its variables; some item keeps exactly 30 and another all 48. `variable_ids`: each item's slots name every variable once.
All inputs are finite; a program needn't handle non-finite values.
Results may differ from a plain program's by a relative error of at most 0.017.
Values may be sent and summed in bfloat16 or wider, within the bound.
A program may use at most 320 MiB of HBM per device.

v0:
```python
from functools import partial
import math

import jax
import jax.numpy as jnp
from jax import lax
from jax.sharding import PartitionSpec as P

D = 1024
HEADS = 16
HDIM = 64
NVAR = 48
NOUT = 48
LATP = 32
LONP_DEV = 4
MICRO = 2


HIGH = lax.Precision.HIGHEST
EPSILON = 1e-06
FLOAT = jnp.float32
HALF = jnp.bfloat16


def from_behind(array, axis, by):
    count = lax.axis_size(axis)
    return lax.ppermute(array, axis, [(i, (i + by) % count) for i in range(count)])


def for_sending(array):
    return jax.tree.map(lambda a: a.astype(jnp.bfloat16) if a.dtype == jnp.float32 else a, array)


def product(left, right):
    return jnp.dot(left, right, preferred_element_type=FLOAT)


def exact(left, right):
    return jnp.dot(left, right, precision=HIGH)


def to_tokens(canvas):
    shaped = canvas.reshape(
        canvas.shape[0], canvas.shape[1], canvas.shape[2] // 2, 2, canvas.shape[3] // 2, 2
    )
    return shaped.transpose(2, 4, 0, 1, 3, 5).reshape(-1, canvas.shape[1], 4)


def from_tokens(token_rows, channels):
    shaped = token_rows.reshape(LONP_DEV, LATP, -1, channels, 2, 2)
    return shaped.transpose(2, 3, 0, 4, 1, 5).reshape(-1, channels, 2 * LONP_DEV, 2 * LATP)


def normalize(values):
    centred = values - jnp.mean(values, axis=-1, keepdims=True)
    inverse = lax.rsqrt(jnp.mean(centred * centred, axis=-1, keepdims=True) + EPSILON)
    return (centred * inverse, inverse)


def norm_back(upstream, normal, inverse, scaler):
    weighted = upstream * scaler
    return inverse * (
        weighted
        - jnp.mean(weighted, axis=-1, keepdims=True)
        - normal * jnp.mean(weighted * normal, axis=-1, keepdims=True)
    )


def split_heads(tensor):
    return tensor.reshape(tensor.shape[0], tensor.shape[1], HEADS, HDIM)


def block_scores(query_heads, key_rows):
    return jnp.einsum(
        "qihe,kihe->ihqk", query_heads, split_heads(key_rows), preferred_element_type=FLOAT
    ) * HDIM ** (-0.5)


def key_blocks(complete):
    block_size = math.gcd(complete.shape[0], 256)
    return complete.reshape(
        complete.shape[0] // block_size, block_size, complete.shape[1], complete.shape[2]
    )


def grad_block(query_heads, upstream_heads, log_total, row_delta, key_block):
    probability = jnp.exp(block_scores(query_heads, key_block[:, :, :D]) - log_total[..., None])
    dprobs = jnp.einsum(
        "qihe,kihe->ihqk",
        upstream_heads,
        split_heads(key_block[:, :, D:]),
        preferred_element_type=FLOAT,
    )
    dscores = (probability * (dprobs - row_delta[..., None])).astype(HALF)
    return (probability.astype(HALF), dscores)


def per_device(
    fields,
    variable_ids,
    variable_mask,
    position,
    patching,
    tagging,
    beacon,
    keying,
    valuing,
    lifting,
    merging,
    offset,
    scaling,
    centre,
    projecting,
    biasing,
    mixing,
    nudging,
    rescaling,
    recentre,
    widening,
    uplift,
    narrowing,
    settle,
    reading,
    baseline,
    cotangent,
):
    item_rows = LONP_DEV * LATP
    factor = HDIM ** (-0.5)
    fields_edge, tangent_edge = from_behind(
        (fields[:, :, -1:, :], cotangent[:, :, -1:, :]), "lon", 1
    )
    fields_ext = jnp.concatenate([fields_edge, fields[:, :, :-1, :]], axis=2).astype(FLOAT)
    tangent_ext = jnp.concatenate([tangent_edge, cotangent[:, :, :-1, :]], axis=2)
    selector_all = (
        variable_ids[:, :, None] == jnp.arange(NVAR, dtype=jnp.int32)[None, None, :]
    ).astype(FLOAT)
    mask_all = variable_mask.astype(FLOAT)
    patching_f = patching.astype(FLOAT)
    tagging_f = tagging.astype(FLOAT)
    beacon_f = beacon.astype(FLOAT)
    keying_f = keying.astype(FLOAT)
    scaling_f = scaling.astype(FLOAT)
    rescaling_f = rescaling.astype(FLOAT)
    patch_rows = patching_f.reshape(D, NVAR, 4).transpose(1, 2, 0)
    keymap = jnp.einsum(
        "dhe,he->dh",
        keying_f.reshape(D, HEADS, HDIM),
        beacon_f.reshape(HEADS, HDIM),
        precision=HIGH,
    )
    patch_map = exact(patching_f.T, keymap).reshape(NVAR, 4, HEADS)
    tag_map = exact(tagging_f.T, keymap)
    joint_bias = jnp.concatenate(
        [biasing[:D].astype(FLOAT), jnp.zeros((D,), FLOAT), biasing[D:].astype(FLOAT)]
    )
    count = fields.shape[0] // MICRO
    predicted_parts = []
    slot_parts = []
    running_grads = None
    for section in range(MICRO):
        first = section * count
        selector = selector_all[first : first + count]
        fields_part = fields_ext[first : first + count]
        tangent_part = tangent_ext[first : first + count]
        all_rows = item_rows * count
        ordered = jnp.einsum("isv,iswh->ivwh", selector, fields_part, precision=HIGH)
        present = (
            jnp.einsum("is,isv->iv", mask_all[first : first + count], selector, precision=HIGH)
            > 0.5
        )
        present_rows = jnp.broadcast_to(present[None], (item_rows, count, NVAR)).reshape(
            all_rows, NVAR
        )
        patches = to_tokens(ordered)
        logits = (
            jnp.einsum("tvk,vkh->thv", patches, patch_map, precision=HIGH) + tag_map.T[None]
        ) * factor
        logits = jnp.where(present_rows[:, None, :], logits, -1e30)
        weights = jax.nn.softmax(logits, axis=-1)
        embeds = tagging_f.T[None]
        for corner in range(4):
            embeds = embeds + patches[:, :, corner, None] * patch_rows[None, :, corner, :]
        mixture = jnp.einsum("thv,tvd->thd", weights, embeds, precision=HIGH)
        mixture_low = mixture.astype(HALF)
        pooled = jnp.einsum(
            "thd,dhe->the",
            mixture_low,
            valuing.reshape(D, HEADS, HDIM),
            preferred_element_type=FLOAT,
        ).reshape(all_rows, D) + lifting.astype(FLOAT)
        pooled_low = pooled.astype(HALF)
        placed = position.reshape(item_rows, 1, D).reshape(all_rows, D).astype(FLOAT)
        embedded = product(pooled_low, merging) + offset.astype(FLOAT) + placed
        normal_one, inverse_one = normalize(embedded)
        normed_low = (normal_one * scaling_f + centre.astype(FLOAT)).astype(HALF)
        joint_rows = (
            (product(normed_low, projecting) + joint_bias)
            .astype(HALF)
            .reshape(item_rows, count, 3 * D)
        )
        query_heads = split_heads(joint_rows[:, :, :D])
        key_values = joint_rows[:, :, D:]
        gathered = lax.all_gather(key_values, "lon", axis=0, tiled=True)
        blocks_all = key_blocks(gathered)

        def stats_step(running, key_block):
            highest_now, totals = running
            scores = block_scores(query_heads, key_block[:, :, :D])
            highest = jnp.maximum(highest_now, jnp.max(scores, axis=-1))
            totals = totals * jnp.exp(highest_now - highest) + jnp.sum(
                jnp.exp(scores - highest[..., None]), axis=-1
            )
            return ((highest, totals), None)

        stats_init = (
            jnp.full((count, HEADS, item_rows), -jnp.inf, FLOAT),
            jnp.zeros((count, HEADS, item_rows), FLOAT),
        )
        (highest, totals), ignored = lax.scan(stats_step, stats_init, blocks_all)
        log_total = highest + jnp.log(totals)

        def output_step(running, key_block):
            probability = jnp.exp(
                block_scores(query_heads, key_block[:, :, :D]) - log_total[..., None]
            )
            return (
                running
                + jnp.einsum(
                    "ihqk,kihe->qihe",
                    probability.astype(HALF),
                    split_heads(key_block[:, :, D:]),
                    preferred_element_type=FLOAT,
                ),
                None,
            )

        zeros_heads = jnp.zeros((item_rows, count, HEADS, HDIM), FLOAT)
        attended, ignored = lax.scan(output_step, zeros_heads, blocks_all)
        attended_low = attended.reshape(all_rows, D).astype(HALF)
        middle = embedded + (product(attended_low, mixing) + nudging.astype(FLOAT))
        normal_two, inverse_two = normalize(middle)
        second_low = (normal_two * rescaling_f + recentre.astype(FLOAT)).astype(HALF)
        hidden = product(second_low, widening) + uplift.astype(FLOAT)
        activated, gelu_pull = jax.vjp(partial(jax.nn.gelu, approximate=True), hidden)
        activated_low = activated.astype(HALF)
        final_rows = middle + (product(activated_low, narrowing) + settle.astype(FLOAT))
        final_low = final_rows.astype(HALF)
        outputs = product(final_low, reading) + baseline.astype(FLOAT)
        predicted = from_tokens(outputs, NOUT).astype(HALF)
        dpred = to_tokens(tangent_part).reshape(all_rows, NOUT * 4)
        baseline_local = jnp.sum(dpred.astype(FLOAT), axis=0)
        reading_grad = product(final_low.T, dpred)
        dfinal = product(dpred, reading.T)
        dfinal_low = dfinal.astype(HALF)
        settle_grad = jnp.sum(dfinal_low.astype(FLOAT), axis=0)
        narrowing_grad = product(activated_low.T, dfinal_low)
        dhidden = gelu_pull(product(dfinal_low, narrowing.T))[0].astype(HALF)
        uplift_grad = jnp.sum(dhidden.astype(FLOAT), axis=0)
        widening_grad = product(second_low.T, dhidden)
        dsecond = product(dhidden, widening.T)
        rescaling_grad = jnp.sum(dsecond * normal_two, axis=0)
        recentre_grad = jnp.sum(dsecond, axis=0)
        dmiddle = dfinal + norm_back(dsecond, normal_two, inverse_two, rescaling_f)
        dmiddle_low = dmiddle.astype(HALF)
        nudging_grad = jnp.sum(dmiddle_low.astype(FLOAT), axis=0)
        mixing_grad = product(attended_low.T, dmiddle_low)
        upstream = split_heads(
            product(dmiddle_low, mixing.T).astype(HALF).reshape(item_rows, count, D)
        )
        row_delta = jnp.einsum("qihe,qihe->ihq", upstream.astype(FLOAT), attended)

        def partial_step(running, key_block):
            probs_low, dscores = grad_block(query_heads, upstream, log_total, row_delta, key_block)
            running = running + jnp.einsum(
                "ihqk,kihe->qihe",
                dscores,
                split_heads(key_block[:, :, :D]),
                preferred_element_type=FLOAT,
            )
            key_grad = (
                jnp.einsum("ihqk,qihe->kihe", dscores, query_heads, preferred_element_type=FLOAT)
                * factor
            )
            value_grad = jnp.einsum(
                "ihqk,qihe->kihe", probs_low, upstream, preferred_element_type=FLOAT
            )
            rows_here = key_block.shape[0]
            return (
                running,
                jnp.concatenate(
                    [
                        key_grad.reshape(rows_here, count, D),
                        value_grad.reshape(rows_here, count, D),
                    ],
                    axis=-1,
                ),
            )

        query_total, partial_terms = lax.scan(partial_step, zeros_heads, key_blocks(gathered))
        key_value_grad = lax.psum_scatter(
            partial_terms.reshape(-1, count, 2 * D).astype(jnp.bfloat16),
            "lon",
            scatter_dimension=0,
            tiled=True,
        ).astype(jnp.float32)
        query_grad = (query_total * factor).reshape(item_rows, count, D)
        djoint = (
            jnp.concatenate([query_grad, key_value_grad], axis=-1)
            .reshape(all_rows, 3 * D)
            .astype(HALF)
        )
        djoint_f = djoint.astype(FLOAT)
        biasing_grad = jnp.concatenate(
            [jnp.sum(djoint_f[:, :D], axis=0), jnp.sum(djoint_f[:, 2 * D :], axis=0)]
        )
        projecting_grad = product(normed_low.T, djoint)
        dnormed = product(djoint, projecting.T)
        scaling_grad = jnp.sum(dnormed * normal_one, axis=0)
        centre_grad = jnp.sum(dnormed, axis=0)
        dembedded = dmiddle + norm_back(dnormed, normal_one, inverse_one, scaling_f)
        position_local = jnp.sum(dembedded.reshape(LONP_DEV, LATP, count, D), axis=2)
        dembedded_low = dembedded.astype(HALF)
        offset_grad = jnp.sum(dembedded_low.astype(FLOAT), axis=0)
        merging_grad = product(pooled_low.T, dembedded_low)
        dpooled = product(dembedded_low, merging.T).astype(HALF)
        lifting_grad = jnp.sum(dpooled.astype(FLOAT), axis=0)
        dpooled_heads = dpooled.reshape(all_rows, HEADS, HDIM)
        valuing_grad = jnp.einsum(
            "thd,the->dhe", mixture_low, dpooled_heads, preferred_element_type=FLOAT
        ).reshape(D, D)
        dmixture = jnp.einsum(
            "the,dhe->thd",
            dpooled_heads,
            valuing.reshape(D, HEADS, HDIM),
            preferred_element_type=FLOAT,
        )
        dweights = jnp.einsum("thd,tvd->thv", dmixture, embeds, precision=HIGH)
        dembeds = jnp.einsum("thv,thd->tvd", weights, dmixture, precision=HIGH)
        patching_grad = jnp.einsum("tvd,tvk->dvk", dembeds, patches, precision=HIGH).reshape(
            D, NVAR * 4
        )
        tagging_grad = jnp.sum(dembeds, axis=0).T
        dlogits = (
            weights * (dweights - jnp.sum(weights * dweights, axis=-1, keepdims=True)) * factor
        )
        dpatches = jnp.einsum("tvd,vkd->tvk", dembeds, patch_rows, precision=HIGH) + jnp.einsum(
            "thv,vkh->tvk", dlogits, patch_map, precision=HIGH
        )
        dpatch_map = jnp.einsum("tvk,thv->vkh", patches, dlogits, precision=HIGH).reshape(
            NVAR * 4, HEADS
        )
        dtag_map = jnp.sum(dlogits, axis=0).T
        patching_grad = patching_grad + exact(keymap, dpatch_map.T)
        tagging_grad = tagging_grad + exact(keymap, dtag_map.T)
        dkeymap = exact(patching_f, dpatch_map) + exact(tagging_f, dtag_map)
        keying_grad = (dkeymap[:, :, None] * beacon_f.reshape(HEADS, HDIM)[None]).reshape(D, D)
        beacon_grad = jnp.einsum(
            "dh,dhe->he", dkeymap, keying_f.reshape(D, HEADS, HDIM), precision=HIGH
        ).reshape(D)
        slot_grad = jnp.einsum(
            "isv,ivwh->iswh", selector, from_tokens(dpatches, NVAR), precision=HIGH
        )
        grads = (
            patching_grad,
            tagging_grad,
            beacon_grad,
            keying_grad,
            valuing_grad,
            lifting_grad,
            merging_grad,
            offset_grad,
            scaling_grad,
            centre_grad,
            projecting_grad,
            biasing_grad,
            mixing_grad,
            nudging_grad,
            rescaling_grad,
            recentre_grad,
            widening_grad,
            uplift_grad,
            narrowing_grad,
            settle_grad,
            reading_grad,
            position_local,
            baseline_local,
        )
        predicted, slot_grad, grads = (predicted, slot_grad, grads)
        predicted_parts.append(predicted)
        slot_parts.append(slot_grad)
        running_grads = (
            grads if running_grads is None else jax.tree.map(jnp.add, running_grads, grads)
        )
    predicted_all = jnp.concatenate(predicted_parts, axis=0)
    slot_all = jnp.concatenate(slot_parts, axis=0)
    folded = from_behind(predicted_all[:, :, :1, :], "lon", -1)
    prediction = jnp.concatenate([predicted_all[:, :, 1:, :], folded], axis=2)
    returned = from_behind(slot_all[:, :, :1, :], "lon", -1)
    fields_gradient = jnp.concatenate([slot_all[:, :, 1:, :], returned], axis=2)
    position_gradient = jax.tree.map(
        lambda part: part.astype(jnp.float32), lax.psum(for_sending(running_grads[21]), "batch")
    )
    summed = lax.psum_scatter(
        tuple(running_grads[:21]), ("batch", "lon"), scatter_dimension=0, tiled=True
    )
    baseline_gradient = lax.psum(running_grads[22], ("batch", "lon"))
    return (prediction, fields_gradient, position_gradient) + tuple(summed) + (baseline_gradient,)


def solution(mesh):
    placed = (
        P("batch", None, "lon", None),
        P("batch", None),
        P("batch", None),
        P("lon", None, None),
        P(),
        P(),
        P(),
        P(),
        P(),
        P(),
        P(),
        P(),
        P(),
        P(),
        P(),
        P(),
        P(),
        P(),
        P(),
        P(),
        P(),
        P(),
        P(),
        P(),
        P(),
        P(),
        P("batch", None, "lon", None),
    )
    return jax.shard_map(
        per_device,
        mesh=mesh,
        in_specs=placed,
        out_specs=(
            P("batch", None, "lon", None),
            P("batch", None, "lon", None),
            P("lon", None, None),
            P(("batch", "lon"), None),
            P(("batch", "lon"), None),
            P(("batch", "lon")),
            P(("batch", "lon"), None),
            P(("batch", "lon"), None),
            P(("batch", "lon")),
            P(("batch", "lon"), None),
            P(("batch", "lon")),
            P(("batch", "lon")),
            P(("batch", "lon")),
            P(("batch", "lon"), None),
            P(("batch", "lon")),
            P(("batch", "lon"), None),
            P(("batch", "lon")),
            P(("batch", "lon")),
            P(("batch", "lon")),
            P(("batch", "lon"), None),
            P(("batch", "lon")),
            P(("batch", "lon"), None),
            P(("batch", "lon")),
            P(("batch", "lon"), None),
            P(),
        ),
        check_vma=False,
    )
```

profile of v0, /device:TPU:14, one launch (start us, length us, event | category | flops | bytes accessed | tf_op | source)
XLA Modules:
  0.0 2005.7 jit_solution(6036475637597552333)
XLA Ops:
  40.4 22.1 %fusion.114 = bf16[128,16,1024]{2,1,0:T(8,128)(2,1)S(1)} fusion(f32[128,16,48]{2,1,0:T(8,128)S(1)} %copy.272, f32[48,1024]{1,0:T(8,128)} %bitcast.772, f32[128,48]{1,0:T(8,128)} %get-tuple-element.738, f32[48,1024]{1,0:T(8,128)} %bitcast.776, f32[128,48]{1,0:T(8,128)} %get-tuple-element.739, f32[48,1024]{1,0:T(8,128)} %bitcast.780, ...), kind=kOutput, calls=%fused_computation.156 | convolution fusion | flops 1260388352 | bytes 5668864 | tf_op jit(solution)/shard_map/thv,tvd->thd/dot_general | solution.py:183
  65.5 21.5 %fusion.115 = bf16[128,16,1024]{2,1,0:T(8,128)(2,1)S(1)} fusion(f32[128,16,48]{2,1,0:T(8,128)S(1)} %copy-done.42, f32[128,48]{1,0:T(8,128)S(1)} %copy-done.150, f32[128,48]{1,0:T(8,128)S(1)} %copy-done.152, f32[128,48]{1,0:T(8,128)S(1)} %copy-done.154, f32[128,48]{1,0:T(8,128)S(1)} %copy-done.148, f32[48,1024]{1,0:T(8,128)S(1)} %bitcast.773, ...), kind=kOutput, calls=%fused_computation.157 | convolution fusion | flops 1260388352 | bytes 5668864 | tf_op jit(solution)/shard_map/thv,tvd->thd/dot_general | solution.py:183
  115.0 16.1 all-gather.5.cloned.1.call-done
  137.4 9.2 while.76
  146.7 19.6 while.77
  176.1 12.9 while.74
  189.1 20.4 %while.75 = (s32[]{:T(128)}, f32[128,1,16,64]{0,3,2,1:T(8,128)}, bf16[4,256,1,2048]{1,3,2,0:T(8,128)(2,1)}, bf16[128,1,16,64]{0,3,2,1:T(8,128)(2,1)}, f32[1,16,128]{2,1,0:T(8,128)S(1)}, /*index=5*/s32[]{:T(128)}, s32[]{:T(128)}) while((s32[]{:T(128)}, f32[128,1,16,64]{0,3,2,1:T(8,128)}, bf16[4,256,1,2048]{1,3,2,0:T(8,128)(2,1)}, ...), condition=%wide.region_9.10_spmd.clone, body=%wide.region_8.9_spmd.clone.sunk | while | flops 136052736 | bytes 6561891 | solution.py:238
  218.1 8.4 convert_reduce_fusion.1
  256.1 51.8 %while.78 = (s32[]{:T(128)}, f32[128,1,16,64]{0,3,2,1:T(8,128)}, bf16[4,256,1,2048]{3,1,0,2:T(8,128)(2,1)}, bf16[4,256,1,2048]{1,3,2,0:T(8,128)(2,1)}, bf16[128,...) while((s32[]{:T(128)}, f32[128,1,16,64]{0,3,2,1:T(8,128)}, ...), condition=%wide.region_27.28_spmd.clone, body=%wide.region_26.27_spmd.clone.sunk | while | flops 342622208 | bytes 24666240 | solution.py:299
  310.5 44.4 %while.79 = (s32[]{:T(128)}, f32[128,1,16,64]{0,3,2,1:T(8,128)}, bf16[4,256,1,2048]{3,1,0,2:T(8,128)(2,1)}, bf16[4,256,1,2048]{1,3,2,0:T(8,128)(2,1)}, bf16[128,...) while((s32[]{:T(128)}, f32[128,1,16,64]{0,3,2,1:T(8,128)}, ...), condition=%wide.region_35.36_spmd.clone, body=%wide.region_34.35_spmd.clone.sunk | while | flops 342622208 | bytes 24666240 | solution.py:299
  372.8 7.4 multiply_reduce_fusion.3
  380.2 34.2 %reduce-scatter.17.cloned.1.call-done = bf16[128,1,2048]{2,0,1:T(8,128)(2,1)} async-done(((bf16[1024,1,2048]{2,0,1:T(8,128)(2,1)}), bf16[128,1,2048]{2,0,1:T(8,128)(2,1)}) %reduce-scatter.17.cloned.1.call-update) | async-done | bytes 524304 | tf_op jit(solution)/shard_map/reduce_scatter | solution.py:300
  435.2 31.8 %fusion.48 = f32[128,16,48]{2,1,0:T(8,128)} fusion(f32[128,48]{1,0:T(8,128)S(1)} %copy-done.151, f32[128,48]{1,0:T(8,128)S(1)} %copy-done.153, f32[128,48]{1,0:T(8,128)S(1)} %copy-done.155, f32[128,48]{1,0:T(8,128)S(1)} %copy-done.149, f32[48,1024]{1,0:T(8,128)S(1)} %bitcast.774, f32[48,1024]{1,0:T(8,128)S(1)} %bitcast.778, f32[48,1024]{1,0:T(8,128)S(1)} %bitcast.782, ...), kind=kOutput, calls=%fused_computation.75 | convolution fusion | flops 1258291200 | bytes 9863168 | tf_op jit(solution)/shard_map/thd,tvd->thv/dot_general | solution.py:337
  467.1 26.4 %fusion.256 = (f32[48,1024]{1,0:T(8,128)}, f32[128,48,1024]{2,1,0:T(8,128)}) fusion(f32[128,16,48]{2,1,0:T(8,128)S(1)} %copy-done.43, f32[128,16,1024]{2,0,1:T(8,128)S(1)} %convolution_bitcast_fusion.2), kind=kOutput, calls=%fused_computation.431 | convolution fusion | flops 1214201856 | bytes 34144256 | tf_op jit(solution)/shard_map/thv,thd->tvd/dot_general | solution.py:338
  497.8 32.4 %fusion.50 = f32[128,16,48]{2,1,0:T(8,128)} fusion(f32[48,1024]{1,0:T(8,128)S(1)} %bitcast.775, f32[128,48]{1,0:T(8,128)S(1)} %copy-done.145, f32[48,1024]{1,0:T(8,128)S(1)} %bitcast.779, f32[128,48]{1,0:T(8,128)S(1)} %copy-done.146, f32[48,1024]{1,0:T(8,128)S(1)} %bitcast.783, f32[128,48]{1,0:T(8,128)S(1)} %copy-done.147, f32[48,1024]{1,0:T(8,128)S(1)} %bitcast.771, ...), kind=kOutput, calls=%fused_computation.78 | convolution fusion | flops 1258291200 | bytes 9863168 | tf_op jit(solution)/shard_map/thd,tvd->thv/dot_general | solution.py:337
  530.2 26.1 %fusion.257 = (f32[48,1024]{1,0:T(8,128)}, f32[128,48,1024]{2,1,0:T(8,128)}) fusion(f32[128,16,48]{2,1,0:T(8,128)S(1)} %copy-done.41, f32[128,16,1024]{2,0,1:T(8,128)S(1)} %convolution_bitcast_fusion.3), kind=kOutput, calls=%fused_computation.432 | convolution fusion | flops 1214201856 | bytes 34144256 | tf_op jit(solution)/shard_map/thv,thd->tvd/dot_general | solution.py:338
  566.3 33.5 %fusion.134 = f32[1024,48,4]{0,2,1:T(4,128)S(1)} fusion(f32[128,48,4]{0,2,1:T(4,128)S(1)} %copy-done.84, f32[128,48,1024]{2,1,0:T(8,128)} %get-tuple-element.778), kind=kOutput, calls=%fused_computation.183 | convolution fusion | flops 301989888 | bytes 26050560 | tf_op jit(solution)/shard_map/tvd,tvk->dvk/dot_general | solution.py:339
  605.5 33.2 %fusion.137 = f32[1024,48,4]{0,2,1:T(4,128)S(1)} fusion(f32[128,48,4]{0,2,1:T(4,128)S(1)} %copy-done.82, f32[128,48,1024]{2,1,0:T(8,128)} %get-tuple-element.776), kind=kOutput, calls=%fused_computation.184 | convolution fusion | flops 301989888 | bytes 26050560 | tf_op jit(solution)/shard_map/tvd,tvk->dvk/dot_general | solution.py:339
  652.7 7.3 fusion.102
  701.3 8.2 convolution_add_fusion
  713.4 8.4 convolution_add_fusion.1
  728.3 30.9 %fusion.158 = f32[128,48,4]{0,2,1:T(4,128)S(1)} fusion(f32[128,48,1024]{2,1,0:T(8,128)} %get-tuple-element.776, bf16[1024,48,4]{0,2,1:T(4,128)(2,1)S(1)} %copy-done.39), kind=kOutput, calls=%fused_computation.219 | convolution fusion | flops 301989888 | bytes 25657344 | tf_op jit(solution)/shard_map/tvd,vkd->tvk/dot_general | solution.py:346
  760.0 31.1 %fusion.155 = f32[128,48,4]{0,2,1:T(4,128)S(1)} fusion(f32[128,48,1024]{2,1,0:T(8,128)} %get-tuple-element.778, bf16[1024,48,4]{0,2,1:T(4,128)(2,1)S(1)} %copy-done.39), kind=kOutput, calls=%fused_computation.218 | convolution fusion | flops 301989888 | bytes 25657344 | tf_op jit(solution)/shard_map/tvd,vkd->tvk/dot_general | solution.py:346
  800.8 43.2 %all-reduce.11 = (f32[1024]{0:T(1024)S(1)}, f32[1024]{0:T(1024)S(1)}, f32[1024]{0:T(1024)S(1)}, f32[1024]{0:T(1024)S(1)}, f32[1024]{0:T(1024)S(1)}, /*index=5*/f...) all-reduce(f32[1024]{0:T(1024)S(1)} %add.525, ...), channel_id=6, replica_groups=mesh['batch'=4,'lon'=8] {'batch','lon'}, use_global_device_ids=true, to_apply=%region_47.48.clone | all-reduce | flops 15552 | bytes 124416
  853.1 22.2 %reduce-scatter.19.cloned.1.call-done = f32[32,192]{1,0:T(8,128)} async-done(((f32[1024,192]{1,0:T(8,128)}), f32[32,192]{1,0:T(8,128)}) %reduce-scatter.19.cloned.1.call-update) | async-done | bytes 24592 | tf_op jit(solution)/shard_map/reduce_scatter | solution.py:403
  875.4 139.6 %reduce-scatter.29.cloned.1.call-done = f32[32,1024]{1,0:T(8,128)} async-done(((f32[1024,1024]{1,0:T(8,128)}), f32[32,1024]{1,0:T(8,128)}) %reduce-scatter.29.cloned.1.call-update) | async-done | bytes 131088 | tf_op jit(solution)/shard_map/reduce_scatter | solution.py:403
  1015.0 139.6 %reduce-scatter.23.cloned.1.call-done = f32[32,1024]{1,0:T(8,128)} async-done(((f32[1024,1024]{1,0:T(8,128)}), f32[32,1024]{1,0:T(8,128)}) %reduce-scatter.23.cloned.1.call-update) | async-done | bytes 131088 | tf_op jit(solution)/shard_map/reduce_scatter | solution.py:403
  1154.5 139.6 %reduce-scatter.25.cloned.1.call-done = f32[32,1024]{1,0:T(8,128)} async-done(((f32[1024,1024]{1,0:T(8,128)}), f32[32,1024]{1,0:T(8,128)}) %reduce-scatter.25.cloned.1.call-update) | async-done | bytes 131088 | tf_op jit(solution)/shard_map/reduce_scatter | solution.py:403
  1294.1 139.7 %reduce-scatter.37.cloned.1.call-done = f32[32,1024]{1,0:T(8,128)} async-done(((f32[1024,1024]{1,0:T(8,128)}), f32[32,1024]{1,0:T(8,128)}) %reduce-scatter.37.cloned.1.call-update) | async-done | bytes 131088
  1433.8 190.3 %reduce-scatter.27.cloned.1.call-done = f32[32,3072]{1,0:T(8,128)} async-done(((f32[1024,3072]{1,0:T(8,128)}), f32[32,3072]{1,0:T(8,128)}) %reduce-scatter.27.cloned.1.call-update) | async-done | bytes 393232 | tf_op jit(solution)/shard_map/reduce_scatter | solution.py:403
  1624.1 187.3 %reduce-scatter.33.cloned.1.call-done = f32[128,1024]{1,0:T(8,128)} async-done(((f32[4096,1024]{1,0:T(8,128)}), f32[128,1024]{1,0:T(8,128)}) %reduce-scatter.33.cloned.1.call-update) | async-done | bytes 524304 | tf_op jit(solution)/shard_map/reduce_scatter | solution.py:403
  1811.4 187.3 %reduce-scatter.31.cloned.1.call-done = f32[32,4096]{1,0:T(8,128)} async-done(((f32[1024,4096]{1,0:T(8,128)}), f32[32,4096]{1,0:T(8,128)}) %reduce-scatter.31.cloned.1.call-update) | async-done | bytes 524304 | tf_op jit(solution)/shard_map/reduce_scatter | solution.py:403
  (864 shorter events, 419.1 us)
Async XLA Ops:
  7.2 82.8 %copy-start = (bf16[1024,1024]{1,0:T(8,128)(2,1)S(1)}, bf16[1024,1024]{1,0:T(8,128)(2,1)}, u32[]{:S(2)}) copy-start(bf16[1024,1024]{1,0:T(8,128)(2,1)} %param.49) | copy-start | bytes 6291460
  7.2 123.9 %all-gather.5.cloned.1.call-start = ((), (), s32[]{:S(2)}) async-start(), calls=%async_computation.13 | async-start | bytes 4718592 | tf_op jit(solution)/shard_map/all_gather | solution.py:203
  8.5 23.0 %collective-permute-start = (bf16[2,48,1,64]{1,3,2,0:T(8,128)(2,1)S(1)}, bf16[2,48,1,64]{1,3,2,0:T(8,128)(2,1)S(1)}, u32[]{:S(2)}, u32[]{:S(2)}) collective-permute-start(bf16[2,48,1,64]{1,3,2,0:T(8,128)(2,1)S(1)} %copy.378), channel_id=1, source_target_pairs={{0,1},{1,2},{2,3},{3,4},{4,5},{5,6},{6,7},{7,0},{8,9},{9,10},{10,1... | collective-permute-start | bytes 36872 | tf_op jit(solution)/shard_map/ppermute | solution.py:27
  23.1 74.5 %copy-start.106 = (f32[1024]{0:T(1024)}, f32[1024]{0:T(1024)S(1)}, u32[]{:S(2)}) copy-start(f32[1024]{0:T(1024)S(1)} %convert_element_type.316) | copy-start | bytes 12292
  23.1 74.5 %copy-start.111 = (f32[1024]{0:T(1024)}, f32[1024]{0:T(1024)S(1)}, u32[]{:S(2)}) copy-start(f32[1024]{0:T(1024)S(1)} %convert_element_type.317) | copy-start | bytes 12292
  90.5 76.8 %copy-start.6 = (f32[128,1024]{1,0:T(8,128)}, f32[128,1024]{1,0:T(8,128)S(1)}, u32[]{:S(2)}) copy-start(f32[128,1024]{1,0:T(8,128)S(1)} %get-tuple-element.764) | copy-start | bytes 1572868
  93.8 76.1 %all-gather.3.cloned.1.call-start = ((), (), s32[]{:S(2)}) async-start(), calls=%async_computation.12 | async-start | bytes 4718592 | tf_op jit(solution)/shard_map/all_gather | solution.py:203
  94.0 10.8 collective-permute-start.2
  94.7 146.7 %copy-start.85 = (f32[1024]{0:T(1024)}, f32[1024]{0:T(1024)S(1)}, u32[]{:S(2)}) copy-start(f32[1024]{0:T(1024)S(1)} %convert_element_type.325) | copy-start | bytes 12292
  94.7 135.3 %copy-start.89 = (f32[1024]{0:T(1024)}, f32[1024]{0:T(1024)S(1)}, u32[]{:S(2)}) copy-start(f32[1024]{0:T(1024)S(1)} %convert_element_type.326) | copy-start | bytes 12292
  114.9 257.8 %reduce-scatter.15.cloned.1.call-start = ((), (), s32[]{:S(2)}) async-start(), calls=%async_computation.14 | async-start | bytes 4718592 | tf_op jit(solution)/shard_map/reduce_scatter | solution.py:300
  169.6 71.7 %copy-start.3 = (f32[128,1024]{1,0:T(8,128)}, f32[128,1024]{1,0:T(8,128)S(1)}, u32[]{:S(2)}) copy-start(f32[128,1024]{1,0:T(8,128)S(1)} %get-tuple-element.766) | copy-start | bytes 1572868
  169.6 71.7 %copy-start.158 = (f32[128]{0:T(128)}, f32[128]{0:T(128)S(1)}, u32[]{:S(2)}) copy-start(f32[128]{0:T(128)S(1)} %broadcast_multiply_fusion.8) | copy-start | bytes 1540
  169.9 71.5 %copy-start.162 = (f32[128]{0:T(128)}, f32[128]{0:T(128)S(1)}, u32[]{:S(2)}) copy-start(f32[128]{0:T(128)S(1)} %add_rsqrt_fusion) | copy-start | bytes 1540
  307.9 106.4 %reduce-scatter.17.cloned.1.call-start = ((), (), s32[]{:S(2)}) async-start(), calls=%async_computation.15 | async-start | bytes 4718592 | tf_op jit(solution)/shard_map/reduce_scatter | solution.py:300
  355.0 496.3 %all-reduce.14.cloned.1.call-start = ((), (), s32[]{:S(2)}) async-start(), calls=%async_computation.16 | async-start | bytes 524288 | tf_op jit(solution)/shard_map/psum | solution.py:401
  358.8 331.5 %copy-start.51 = (bf16[128,1,1024]{2,0,1:T(8,128)(2,1)}, bf16[128,1,1024]{2,0,1:T(8,128)(2,1)S(1)}, u32[]{:S(2)}) copy-start(bf16[128,1,1024]{2,0,1:T(8,128)(2,1)S(1)} %copy.311) | copy-start | bytes 786436
  372.7 41.7 %copy-start.184 = (f32[128]{0:T(128)S(1)}, f32[128]{0:T(128)}, u32[]{:S(2)}) copy-start(f32[128]{0:T(128)} %copy-done.183) | copy-start | bytes 1540
  372.7 41.7 %copy-start.188 = (f32[128]{0:T(128)S(1)}, f32[128]{0:T(128)}, u32[]{:S(2)}) copy-start(f32[128]{0:T(128)} %copy-done.187) | copy-start | bytes 1540
  422.4 430.7 %reduce-scatter.35.cloned.1.call-start = ((), (), s32[]{:S(2)}) async-start(), calls=%async_computation.25 | async-start | bytes 1081344 | tf_op jit(solution)/shard_map/reduce_scatter | solution.py:403
  425.1 428.0 %reduce-scatter.21.cloned.1.call-start = ((), (), s32[]{:S(2)}) async-start(), calls=%async_computation.18 | async-start | bytes 540672 | tf_op jit(solution)/shard_map/reduce_scatter | solution.py:403
  638.7 236.6 %reduce-scatter.19.cloned.1.call-start = ((), (), s32[]{:S(2)}) async-start(), calls=%async_computation.17 | async-start | bytes 1081344 | tf_op jit(solution)/shard_map/reduce_scatter | solution.py:403
  647.2 367.8 %reduce-scatter.29.cloned.1.call-start = ((), (), s32[]{:S(2)}) async-start(), calls=%async_computation.22 | async-start | bytes 4325376 | tf_op jit(solution)/shard_map/reduce_scatter | solution.py:403
  651.8 502.7 %reduce-scatter.23.cloned.1.call-start = ((), (), s32[]{:S(2)}) async-start(), calls=%async_computation.19 | async-start | bytes 4325376 | tf_op jit(solution)/shard_map/reduce_scatter | solution.py:403
  672.3 621.8 %reduce-scatter.25.cloned.1.call-start = ((), (), s32[]{:S(2)}) async-start(), calls=%async_computation.20 | async-start | bytes 4325376 | tf_op jit(solution)/shard_map/reduce_scatter | solution.py:403
  676.9 756.9 %reduce-scatter.37.cloned.1.call-start = ((), (), s32[]{:S(2)}) async-start(), calls=%async_computation.26 | async-start | bytes 4325376
  687.3 936.8 %reduce-scatter.27.cloned.1.call-start = ((), (), s32[]{:S(2)}) async-start(), calls=%async_computation.21 | async-start | bytes 12976128 | tf_op jit(solution)/shard_map/reduce_scatter | solution.py:403
  697.0 1114.4 %reduce-scatter.33.cloned.1.call-start = ((), (), s32[]{:S(2)}) async-start(), calls=%async_computation.24 | async-start | bytes 17301504 | tf_op jit(solution)/shard_map/reduce_scatter | solution.py:403
  709.6 1289.1 %reduce-scatter.31.cloned.1.call-start = ((), (), s32[]{:S(2)}) async-start(), calls=%async_computation.23 | async-start | bytes 17301504 | tf_op jit(solution)/shard_map/reduce_scatter | solution.py:403
  724.7 2.7 collective-permute-start.1
  793.0 57.4 %collective-permute-start.3 = (f32[2,48,1,64]{3,1,2,0:T(8,128)S(1)}, f32[2,48,1,64]{3,1,2,0:T(8,128)S(1)}, u32[]{:S(2)}, u32[]{:S(2)}) collective-permute-start(f32[2,48,1,64]{3,1,2,0:T(8,128)S(1)} %pad_maximum_fusion.4), channel_id=1, source_target_pairs={{0,7},{1,0},{2,1},{3,2},{4,3},{5,4},{6,5},{7,6},{8,15},{9,8},{10,9... | collective-permute-start | bytes 73736 | tf_op jit(solution)/shard_map/ppermute | solution.py:27
  798.8 1199.9 %copy-start.1 = (bf16[1024,1024]{1,0:T(8,128)(2,1)S(1)}, bf16[1024,1024]{1,0:T(8,128)(2,1)}, u32[]{:S(2)}) copy-start(bf16[1024,1024]{1,0:T(8,128)(2,1)} %param.49) | copy-start | bytes 6291460
  (200 other events, 1270.2 us)
Sparse Core Ops, SparseCore 0:
  93.9 37.1 all-gather.4
  133.0 36.7 all-gather.2
  308.1 51.3 reduce-scatter.14
  363.0 51.3 reduce-scatter.16
  422.5 36.1 all-reduce.13
  461.5 102.2 reduce-scatter.34
  638.9 102.5 reduce-scatter.20
  744.3 130.9 reduce-scatter.18
  878.2 136.7 reduce-scatter.28
  1017.7 136.8 reduce-scatter.22
  1157.4 136.6 reduce-scatter.24
  1296.8 136.9 reduce-scatter.36
  1440.4 183.6 reduce-scatter.26
  1626.9 184.3 reduce-scatter.32
  1814.2 184.4 reduce-scatter.30
where the time goes:
time: 2020 us; the launch traced here: 2010 us
  waiting for transfers between devices  1200 us (59%)
  matrix products  547 us (27%)
  local copies, waits for them, and re-layouts  158 us (8%)
  blocking collectives  43.2 us (2%)
  other arithmetic  35.3 us (2%)
    reduce_scatter x9, waiting for transfers between devices, per_device(): lax.psum_scatter(tuple(running_grads[:21]), ('batch', 'lon'), scatter_dim...  1010 us
    unnamed x16, waiting for transfers between devices  140 us
    dot_general x36, matrix products, product(): return jnp.dot(left, right, preferred_element_type=FLOAT)  119 us
    dot_general x2, matrix products, per_device(): jnp.einsum('tvd,tvk->dvk', dembeds, patches, precision=HIGH)  66.7 us
    dot_general x2, matrix products, per_device(): dweights = jnp.einsum('thd,tvd->thv', dmixture, embeds, precision=HIGH)  64.2 us
    dot_general x2, matrix products, per_device(): jnp.einsum('tvd,vkd->tvk', dembeds, patch_rows, precision=HIGH)  62 us
    dot_general x2, matrix products, per_device(): dembeds = jnp.einsum('thv,thd->tvd', weights, dmixture, precision=HIGH)  52.5 us
    unnamed x452, local copies, waits for them, and re-layouts  51.7 us
  transfers between devices with their start and end apart: 19, of which 11 were waited for; matrix products, arithmetic and copies ran while one was open for 26% of the time, Pallas kernels for 0%

commit v1 on v0

v1 whole, which is shorter than its diff:
```python
import functools

import jax
import jax.numpy as jnp
from jax import lax
from jax.experimental import pallas as pl
from jax.experimental.pallas import tpu as pltpu
from jax.sharding import PartitionSpec as P

D = 1024
HEADS = 16
HDIM = 64
FF = 4096
NVAR = 48
NOUT = 48
LATP = 32
VPAD = 64
JPAD = 5 * VPAD

HIGH = lax.Precision.HIGHEST
EPSILON = 1e-06
F32 = jnp.float32
BF16 = jnp.bfloat16
FACTOR = HDIM ** (-0.5)
MIB = 2**20


def product(left, right):
    return jnp.dot(left, right, preferred_element_type=F32)


def contract(left, right, dims):
    return lax.dot_general(left, right, (dims, ((), ())), preferred_element_type=F32)


def normalize(values):
    centred = values - jnp.mean(values, axis=-1, keepdims=True)
    inverse = lax.rsqrt(jnp.mean(centred * centred, axis=-1, keepdims=True) + EPSILON)
    return centred * inverse, inverse


def norm_back(upstream, normal, inverse, scaler):
    weighted = upstream * scaler
    return inverse * (
        weighted
        - jnp.mean(weighted, axis=-1, keepdims=True)
        - normal * jnp.mean(weighted * normal, axis=-1, keepdims=True)
    )


def gelu_parts(x):
    c = 0.7978845608028654
    t = jnp.tanh(c * (x + 0.044715 * (x * x * x)))
    value = 0.5 * x * (1.0 + t)
    slope = 0.5 * (1.0 + t) + 0.5 * x * (1.0 - t * t) * (c * (1.0 + 3 * 0.044715 * x * x))
    return value, slope


def pool_weights(patches_ref, logit_map_ref, tag_row_ref, mask_ref, weights):
    logits = jnp.dot(
        patches_ref[...].astype(F32)[:, : 4 * VPAD],
        logit_map_ref[...],
        precision=HIGH,
        preferred_element_type=F32,
    ) + tag_row_ref[...]
    mask = mask_ref[...]
    for h in range(HEADS):
        part = jnp.where(mask == 0.0, logits[:, h * VPAD : (h + 1) * VPAD], mask)
        top = jnp.max(part, axis=-1, keepdims=True)
        grown = jnp.exp(part - top)
        weights[h] = grown / jnp.sum(grown, axis=-1, keepdims=True)


def pool_fwd_kernel(patches_ref, logit_map_ref, tag_row_ref, mask_ref, pv_ref, lift_ref, out_ref, w_ref):
    pool_weights(patches_ref, logit_map_ref, tag_row_ref, mask_ref, w_ref)
    patches = patches_ref[...].astype(F32)
    for pair in range(HEADS // 2):
        halves = []
        for h in (2 * pair, 2 * pair + 1):
            w = w_ref[h]
            blended = (jnp.concatenate([w] * 5, axis=1) * patches).astype(BF16)
            halves.append(product(blended, pv_ref[:, h * HDIM : (h + 1) * HDIM]))
        cols = slice(pair * 128, pair * 128 + 128)
        out_ref[:, cols] = (jnp.concatenate(halves, axis=1) + lift_ref[:, cols]).astype(BF16)


def pool_forward(patches, logit_map, tag_row, mask, pv, lifting):
    rows = patches.shape[0]
    return pl.pallas_call(
        pool_fwd_kernel,
        out_shape=(
            jax.ShapeDtypeStruct((rows, D), BF16),
            jax.ShapeDtypeStruct((HEADS, rows, VPAD), F32),
        ),
        compiler_params=pltpu.CompilerParams(vmem_limit_bytes=48 * MIB),
        name="pool_fwd",
    )(patches, logit_map, tag_row, mask, pv, lifting)


def pool_bwd_kernel(patches_ref, w_ref, qrow_ref, pv_ref, du_ref, dpatch_ref, dpv_ref, dqz_ref):
    patches = patches_ref[...].astype(F32)
    total = jnp.zeros((patches.shape[0], 4 * VPAD), F32)
    for pair in range(HEADS // 2):
        halves = []
        for h in (2 * pair, 2 * pair + 1):
            w = w_ref[h]
            wide = jnp.concatenate([w] * 5, axis=1)
            blended = (wide * patches).astype(BF16)
            du = du_ref[:, h * HDIM : (h + 1) * HDIM]
            dbl = contract(du, pv_ref[:, h * HDIM : (h + 1) * HDIM], ((1,), (1,)))
            halves.append(contract(blended, du, ((0,), (0,))))
            x = dbl * patches
            dw = x[:, :VPAD]
            for k in range(1, 5):
                dw = dw + x[:, k * VPAD : (k + 1) * VPAD]
            da = w * (dw - jnp.sum(w * dw, axis=-1, keepdims=True)) * FACTOR
            da_wide = jnp.concatenate([da] * 5, axis=1)
            dqz_ref[h : h + 1, :] = jnp.sum(da_wide * patches, axis=0, keepdims=True)
            total = total + (
                wide[:, : 4 * VPAD] * dbl[:, : 4 * VPAD]
                + da_wide[:, : 4 * VPAD] * qrow_ref[h : h + 1, : 4 * VPAD]
            )
        dpv_ref[:, pair * 128 : pair * 128 + 128] = jnp.concatenate(halves, axis=1)
    dpatch_ref[...] = total


def pool_backward(patches, weights, qrow, pv, du):
    rows = patches.shape[0]
    return pl.pallas_call(
        pool_bwd_kernel,
        out_shape=(
            jax.ShapeDtypeStruct((rows, 4 * VPAD), F32),
            jax.ShapeDtypeStruct((JPAD, D), F32),
            jax.ShapeDtypeStruct((HEADS, JPAD), F32),
        ),
        compiler_params=pltpu.CompilerParams(vmem_limit_bytes=48 * MIB),
        name="pool_bwd",
    )(patches, weights, qrow, pv, du)


def attn_fwd_kernel(heads, q_ref, k_ref, v_ref, out_ref, lse_ref):
    outs = []
    for h in range(heads):
        cols = slice(h * HDIM, (h + 1) * HDIM)
        scores = contract(k_ref[0, :, cols], q_ref[0, :, cols], ((1,), (1,))) * FACTOR
        top = jnp.max(scores, axis=0, keepdims=True)
        grown = jnp.exp(scores - top)
        total = jnp.sum(grown, axis=0, keepdims=True)
        probs = (grown * (1.0 / total)).astype(BF16)
        outs.append(contract(probs, v_ref[0, :, cols], ((0,), (0,))))
        lse_ref[0, h : h + 1, :] = top + jnp.log(total)
    out_ref[0] = jnp.concatenate(outs, axis=1).astype(BF16) if heads > 1 else outs[0].astype(BF16)


def attn_forward(q, k, v, heads, tile):
    items, seq, width = q.shape
    return pl.pallas_call(
        functools.partial(attn_fwd_kernel, heads),
        grid=(items, seq // tile),
        in_specs=[
            pl.BlockSpec((1, tile, width), lambda i, t: (i, t, 0)),
            pl.BlockSpec((1, seq, width), lambda i, t: (i, 0, 0)),
            pl.BlockSpec((1, seq, width), lambda i, t: (i, 0, 0)),
        ],
        out_specs=(
            pl.BlockSpec((1, tile, width), lambda i, t: (i, t, 0)),
            pl.BlockSpec((1, heads, tile), lambda i, t: (i, 0, t)),
        ),
        out_shape=(
            jax.ShapeDtypeStruct((items, seq, width), BF16),
            jax.ShapeDtypeStruct((items, heads, seq), F32),
        ),
        compiler_params=pltpu.CompilerParams(vmem_limit_bytes=56 * MIB),
        name="attn_fwd",
    )(q, k, v)


def attn_bwd_kernel(heads, q_ref, k_ref, v_ref, do_ref, lse_ref, dq_ref, dk_ref, dv_ref, dk_acc, dv_acc):
    tile = pl.program_id(1)

    @pl.when(tile == 0)
    def _():
        dk_acc[...] = jnp.zeros_like(dk_acc)
        dv_acc[...] = jnp.zeros_like(dv_acc)

    for h in range(heads):
        cols = slice(h * HDIM, (h + 1) * HDIM)
        q, k, v, do = q_ref[0, :, cols], k_ref[0, :, cols], v_ref[0, :, cols], do_ref[0, :, cols]
        scores = contract(k, q, ((1,), (1,))) * FACTOR
        probs = jnp.exp(scores - lse_ref[0, h : h + 1, :])
        dprobs = contract(v, do, ((1,), (1,)))
        delta = jnp.sum(probs * dprobs, axis=0, keepdims=True)
        dscores = (probs * (dprobs - delta)).astype(BF16)
        dv_acc[h] += product(probs.astype(BF16), do)
        dk_acc[h] += product(dscores, q)
        dq_ref[0, :, cols] = (contract(dscores, k, ((0,), (0,))) * FACTOR).astype(BF16)

    @pl.when(tile == pl.num_programs(1) - 1)
    def _():
        for h in range(heads):
            cols = slice(h * HDIM, (h + 1) * HDIM)
            dk_ref[0, :, cols] = (dk_acc[h] * FACTOR).astype(BF16)
            dv_ref[0, :, cols] = dv_acc[h].astype(BF16)


def attn_backward(q, k, v, do, lse, heads, tile):
    items, seq, width = q.shape
    tiled = pl.BlockSpec((1, tile, width), lambda i, t: (i, t, 0))
    full = pl.BlockSpec((1, seq, width), lambda i, t: (i, 0, 0))
    shape = jax.ShapeDtypeStruct((items, seq, width), BF16)
    return pl.pallas_call(
        functools.partial(attn_bwd_kernel, heads),
        grid=(items, seq // tile),
        in_specs=[tiled, full, full, tiled, pl.BlockSpec((1, heads, tile), lambda i, t: (i, 0, t))],
        out_specs=(tiled, full, full),
        out_shape=(shape, shape, shape),
        scratch_shapes=[pltpu.VMEM((heads, seq, HDIM), F32), pltpu.VMEM((heads, seq, HDIM), F32)],
        compiler_params=pltpu.CompilerParams(vmem_limit_bytes=56 * MIB),
        name="attn_bwd",
    )(q, k, v, do, lse)


def per_device(
    fields, variable_ids, variable_mask, position, patching, tagging, beacon, keying, valuing, lifting,
    merging, offset, scaling, centre, projecting, biasing, mixing, nudging, rescaling, recentre,
    widening, uplift, narrowing, settle, reading, baseline, cotangent,
):
    count, lon = lax.axis_size("batch"), lax.axis_size("lon")
    zi, li = lax.axis_index("batch"), lax.axis_index("lon")
    block = zi * lon + li
    items, cols_dev, lat = fields.shape[0], fields.shape[2], fields.shape[3]
    upatch = cols_dev // 2
    here = upatch * LATP
    rows = items * here
    own_heads = HEADS // lon
    width = own_heads * HDIM
    rows_dev = D // (count * lon)
    f = lambda a: a.astype(F32)

    canvas = jnp.stack([fields, cotangent])
    edge = lax.ppermute(canvas[:, :, :, -1:, :], "lon", [(i, (i + 1) % lon) for i in range(lon)])
    canvas = jnp.concatenate([edge, canvas[:, :, :, :-1, :]], axis=3)

    q_at = jnp.arange(lat)
    spread = ((q_at[:, None] % 2) * LATP + q_at[:, None] // 2 == q_at[None, :]).astype(BF16)
    choose = (variable_ids[:, :, None] == jnp.arange(VPAD, dtype=jnp.int32)[None, None, :]).astype(BF16)
    ordered = jnp.einsum("bsv,bswq->bwvq", choose, canvas[0], preferred_element_type=F32).astype(BF16)
    ptok = jnp.einsum("bwvq,qc->bwcv", ordered, spread, preferred_element_type=F32).astype(BF16)
    ptok = ptok.reshape(items, upatch, 2, 2, LATP, VPAD).transpose(0, 1, 4, 2, 3, 5).reshape(rows, 4 * VPAD)
    patches = jnp.concatenate([ptok, jnp.ones((rows, VPAD), BF16)], axis=1)
    ytok = jnp.einsum("bowq,qc->bwco", canvas[1], spread, preferred_element_type=F32).astype(BF16)
    dpred = ytok.reshape(items, upatch, 2, 2, LATP, NOUT).transpose(0, 1, 4, 2, 3, 5).reshape(rows, 4 * NOUT)
    live = jnp.einsum("bs,bsv->bv", variable_mask.astype(BF16), choose, preferred_element_type=F32) > 0.5
    lane = jnp.arange(VPAD)[None, :]
    mask = jnp.where(lane < NVAR, jnp.where(live, 0.0, -1e30), -2e30)
    mask = jnp.broadcast_to(mask[:, None, :], (items, here, VPAD)).reshape(rows, VPAD)

    source = jnp.concatenate([jnp.arange(NVAR * 4) % 4 * VPAD + jnp.arange(NVAR * 4) // 4, 4 * VPAD + jnp.arange(NVAR)])
    place = (source[:, None] == jnp.arange(JPAD)[None, :]).astype(BF16)
    embed = product(jnp.concatenate([patching, tagging], axis=1), place).astype(BF16)
    pv = contract(embed, valuing, ((0,), (0,))).astype(BF16)
    head_of = (jnp.arange(D)[:, None] // HDIM == jnp.arange(HEADS)[None, :])
    keymap = product(keying, jnp.where(head_of, beacon[:, None], jnp.zeros((), BF16)))
    qmap = jnp.dot(f(embed).T, keymap, precision=HIGH)
    same = (jnp.arange(4 * VPAD)[:, None] % VPAD == jnp.arange(VPAD)[None, :])
    logit_map = jnp.where(same[:, None, :], qmap[: 4 * VPAD, :, None], 0.0).reshape(4 * VPAD, HEADS * VPAD) * FACTOR
    tag_row = (qmap[4 * VPAD :, :].T * FACTOR).reshape(1, HEADS * VPAD)

    pooled, pool_w = pool_forward(patches, logit_map, tag_row, mask, pv, f(lifting)[None, :])
    placed = jnp.broadcast_to(f(position).reshape(1, here, D), (items, here, D)).reshape(rows, D)
    embedded = product(pooled, merging) + f(offset) + placed
    normal_one, inverse_one = normalize(embedded)
    normed = (normal_one * f(scaling) + f(centre)).astype(BF16)

    normed_all = lax.all_gather(normed.reshape(items, here, D), "lon", axis=1, tiled=True)
    seq = normed_all.shape[1]
    own = lax.dynamic_slice(projecting.reshape(D, 3, lon, width), (0, 0, li, 0), (D, 3, 1, width)).reshape(D, 3 * width)
    joint_bias = jnp.concatenate([biasing[:D], jnp.zeros((D,), BF16), biasing[D:]]).reshape(3, lon, width)
    own_bias = lax.dynamic_slice(joint_bias, (0, li, 0), (3, 1, width)).reshape(3 * width)
    joint = (product(normed_all.reshape(items * seq, D), own) + f(own_bias)).astype(BF16).reshape(items, seq, 3 * width)
    q, k, v = joint[:, :, :width], joint[:, :, width : 2 * width], joint[:, :, 2 * width :]
    attended, lse = attn_forward(q, k, v, own_heads, 512)

    def heads_to_tokens(a):
        w = a.shape[-1]
        a = lax.all_to_all(a.reshape(items, lon, here, w), "lon", 1, 1, tiled=True)
        return a.transpose(0, 2, 1, 3).reshape(rows, lon * w)

    def tokens_to_heads(a):
        w = a.shape[-1] // lon
        a = lax.all_to_all(a.reshape(items, here, lon, w).transpose(0, 2, 1, 3), "lon", 1, 1, tiled=True)
        return a.reshape(items, seq, w)

    attended_low = heads_to_tokens(attended)
    middle = embedded + (product(attended_low, mixing) + f(nudging))
    normal_two, inverse_two = normalize(middle)
    second = (normal_two * f(rescaling) + f(recentre)).astype(BF16)
    second_all = lax.all_gather(second, "lon", axis=0, tiled=True)
    activated, slope = gelu_parts(product(second, widening) + f(uplift))
    activated = activated.astype(BF16)
    final = (middle + (product(activated, narrowing) + f(settle))).astype(BF16)

    corner = jnp.arange(NOUT * 4)
    shuffle = ((corner % 4) * NOUT + corner // 4)[:, None] == corner[None, :]
    shuffle = shuffle.astype(BF16)
    reading_p = product(reading, shuffle).astype(BF16)
    baseline_p = product(baseline[None, :], shuffle)
    outputs = product(final, reading_p) + baseline_p
    canvas_out = outputs.astype(BF16).reshape(items, upatch, LATP, 2, 2, NOUT).transpose(0, 1, 3, 5, 4, 2)
    canvas_out = canvas_out.reshape(items, cols_dev, NOUT, lat)
    predicted = jnp.einsum("bwoc,qc->bowq", canvas_out, spread, preferred_element_type=F32).astype(BF16)
    folded = lax.ppermute(predicted[:, :, :1, :], "lon", [(i, (i - 1) % lon) for i in range(lon)])
    prediction = jnp.concatenate([predicted[:, :, 1:, :], folded], axis=2)

    baseline_local = jnp.sum(f(dpred), axis=0)
    reading_grad = contract(final, dpred, ((0,), (0,)))
    dfinal = contract(dpred, reading_p, ((1,), (1,)))
    dfinal_low = dfinal.astype(BF16)
    upstream_all = lax.all_gather(dfinal_low, "lon", axis=0, tiled=True)
    settle_local = jnp.sum(f(dfinal_low), axis=0)
    dhidden = (contract(dfinal_low, narrowing, ((1,), (1,))) * slope).astype(BF16)
    uplift_local = jnp.sum(f(dhidden), axis=0)
    dsecond = contract(dhidden, widening, ((1,), (1,)))
    rescaling_local = jnp.sum(dsecond * normal_two, axis=0)
    recentre_local = jnp.sum(dsecond, axis=0)
    dmiddle = dfinal + norm_back(dsecond, normal_two, inverse_two, f(rescaling))
    dmiddle_low = dmiddle.astype(BF16)
    nudging_local = jnp.sum(f(dmiddle_low), axis=0)
    mixing_grad = contract(attended_low, dmiddle_low, ((0,), (0,)))
    dattended = contract(dmiddle_low, mixing, ((1,), (1,))).astype(BF16)

    hid = FF // (count * lon)
    wide_own = lax.dynamic_slice(widening.reshape(D, count, lon, hid), (0, 0, li, 0), (D, count, 1, hid)).reshape(D, count * hid)
    narrow_own = lax.dynamic_slice(narrowing.reshape(count, lon, hid, D), (0, li, 0, 0), (count, 1, hid, D)).reshape(count * hid, D)
    uplift_own = lax.dynamic_slice(uplift.reshape(count, lon, hid), (0, li, 0), (count, 1, hid)).reshape(count * hid)
    value_own, slope_own = gelu_parts(product(second_all, wide_own) + f(uplift_own))
    dhidden_own = (contract(upstream_all, narrow_own, ((1,), (1,))) * slope_own).astype(BF16)
    narrowing_own = contract(value_own.astype(BF16), upstream_all, ((0,), (0,)))
    widening_own = contract(second_all, dhidden_own, ((0,), (0,)))
    narrowing_gradient = f(lax.psum_scatter(narrowing_own.astype(BF16), "batch", scatter_dimension=0, tiled=True))

    do = tokens_to_heads(dattended)
    dq, dk, dv = attn_backward(q, k, v, do, lse, own_heads, 512)
    djoint_own = jnp.concatenate([dq, dk, dv], axis=2)
    projecting_own = contract(normed_all.reshape(items * seq, D), djoint_own.reshape(items * seq, 3 * width), ((0,), (0,)))
    columns_own = jnp.concatenate([widening_own, projecting_own], axis=1).astype(BF16)
    columns_own = lax.psum_scatter(columns_own, "batch", scatter_dimension=0, tiled=True)
    columns_own = lax.all_to_all(columns_own.reshape(lon, rows_dev, -1), "lon", 0, 0, tiled=True)
    widening_gradient = f(columns_own[:, :, : count * hid].reshape(lon, rows_dev, count, hid).transpose(1, 2, 0, 3).reshape(rows_dev, FF))
    projecting_gradient = f(columns_own[:, :, count * hid :].reshape(lon, rows_dev, 3, width).transpose(1, 2, 0, 3).reshape(rows_dev, 3 * D))

    djoint = heads_to_tokens(djoint_own).reshape(rows, lon, 3, width).transpose(0, 2, 1, 3).reshape(rows, 3 * D)
    djoint_sum = jnp.sum(f(djoint), axis=0)
    dnormed = contract(djoint, projecting, ((1,), (1,)))
    scaling_local = jnp.sum(dnormed * normal_one, axis=0)
    centre_local = jnp.sum(dnormed, axis=0)
    dembedded = dmiddle + norm_back(dnormed, normal_one, inverse_one, f(scaling))
    position_local = jnp.sum(dembedded.reshape(items, here, D), axis=0)
    position_gradient = f(lax.psum(position_local.astype(BF16), "batch")).reshape(upatch, LATP, D)
    dembedded_low = dembedded.astype(BF16)
    offset_local = jnp.sum(f(dembedded_low), axis=0)
    merging_grad = contract(pooled, dembedded_low, ((0,), (0,)))
    dpooled = contract(dembedded_low, merging, ((1,), (1,))).astype(BF16)
    lifting_local = jnp.sum(f(dpooled), axis=0)
    dpatch, dpv, dqz = pool_backward(patches, pool_w, qmap.T, pv, dpooled)

    squares = jnp.concatenate([merging_grad, mixing_grad, reading_grad], axis=1).astype(BF16)
    squares = squares.reshape(count, lon, rows_dev, -1)
    squares = lax.psum_scatter(squares, "lon", scatter_dimension=1, tiled=True)
    squares = f(lax.psum_scatter(squares, "batch", scatter_dimension=0, tiled=True)).reshape(rows_dev, -1)
    merging_gradient, mixing_gradient = squares[:, :D], squares[:, D : 2 * D]
    reading_gradient = jnp.dot(squares[:, 2 * D :], f(shuffle).T, precision=HIGH)

    vectors = jnp.concatenate([
        lifting_local, offset_local, scaling_local, centre_local, djoint_sum[:D], djoint_sum[2 * D :],
        nudging_local, rescaling_local, recentre_local, settle_local, uplift_local, baseline_local, dqz.reshape(-1),
    ])
    vectors = lax.psum(lax.psum(vectors, "lon"), "batch")
    dpv = lax.psum(lax.psum(dpv.astype(BF16), "lon"), "batch")
    dqz = vectors[14 * D + 4 * NOUT :].reshape(HEADS, JPAD)

    def mine(a, size):
        return lax.dynamic_slice_in_dim(a, block * size, size, 0)

    vec = lambda i: mine(vectors[i * D : (i + 1) * D], rows_dev)
    biasing_gradient = mine(vectors[4 * D : 6 * D], 2 * rows_dev)
    uplift_gradient = mine(vectors[10 * D : 14 * D], 4 * rows_dev)
    baseline_gradient = jnp.dot(vectors[None, 14 * D : 14 * D + 4 * NOUT], f(shuffle).T, precision=HIGH)[0]

    embed_mine = mine(embed, rows_dev)
    valuing_gradient = product(embed_mine, dpv)
    dembed = contract(mine(valuing, rows_dev), dpv, ((1,), (1,))) + jnp.dot(mine(keymap, rows_dev), dqz, precision=HIGH)
    dembed = jnp.dot(dembed, f(place).T, precision=HIGH)
    patching_gradient, tagging_gradient = dembed[:, : 4 * NVAR], dembed[:, 4 * NVAR :]
    dkeymap = jnp.dot(f(embed), dqz.T, precision=HIGH)
    keying_gradient = jnp.repeat(mine(dkeymap, rows_dev), HDIM, axis=1) * f(beacon)
    beacon_all = jnp.sum(jnp.repeat(dkeymap, HDIM, axis=1) * f(keying), axis=0)
    beacon_gradient = mine(beacon_all, rows_dev)

    dcan = dpatch.reshape(items, upatch, LATP, 2, 2, VPAD).transpose(0, 1, 3, 5, 4, 2).reshape(items, cols_dev, VPAD, lat)
    dslots = jnp.einsum("bwvc,qc->bwvq", dcan, f(spread), precision=HIGH)
    dslots = jnp.einsum("bsv,bwvq->bswq", f(choose), dslots, precision=HIGH)
    returned = lax.ppermute(dslots[:, :, :1, :], "lon", [(i, (i - 1) % lon) for i in range(lon)])
    fields_gradient = jnp.concatenate([dslots[:, :, 1:, :], returned], axis=2)

    return (
        prediction, fields_gradient, position_gradient, patching_gradient, tagging_gradient, beacon_gradient,
        keying_gradient, valuing_gradient, vec(0), merging_gradient, vec(1), vec(2), vec(3), projecting_gradient,
        biasing_gradient, mixing_gradient, vec(6), vec(7), vec(8), widening_gradient, uplift_gradient,
        narrowing_gradient, vec(9), reading_gradient, baseline_gradient,
    )


def solution(mesh):
    both = ("batch", "lon")
    image, matrix, vector = P("batch", None, "lon", None), P(both, None), P(both)
    return jax.shard_map(
        per_device,
        mesh=mesh,
        in_specs=(image, P("batch", None), P("batch", None), P("lon", None, None)) + (P(),) * 22 + (image,),
        out_specs=(
            image, image, P("lon", None, None), matrix, matrix, vector, matrix, matrix, vector, matrix, vector,
            vector, vector, matrix, vector, matrix, vector, vector, vector, matrix, vector, matrix, vector, matrix, P(),
        ),
        check_vma=False,
    )
```

time: 2020 us -> 662 us (0.33)
  waiting for transfers between devices: 1200 us -> 336 us
  matrix products: 547 us -> 110 us
  local copies, waits for them, and re-layouts: 158 us -> 94.5 us
  blocking collectives: 43.2 us -> 0 us
  Pallas kernels: 0 us -> 42.2 us
    reduce_scatter x11 -> x3, waiting for transfers between devices: 1040 us -> 73.2 us  [the longest x1 41 us: per_device(): lax.psum_scatter(columns_own, 'batch', scatter_dimension=0, tiled=True)]
    dot_general x133 -> x38, matrix products: 547 us -> 110 us  [the longest x14 59.7 us: contract(): lax.dot_general(left, right, (dims, ((), ())), preferred_element_type=F32)]
    psum x1 -> x4, waiting for transfers between devices: 0.01 us -> 170 us  [the longest x1 94.9 us: per_device(): dpv = lax.psum(lax.psum(dpv.astype(BF16), 'lon'), 'batch')]
    unnamed x16 -> x10, waiting for transfers between devices: 140 us -> 1.19 us
    all_gather x2 -> x3, waiting for transfers between devices: 16.2 us -> 86.3 us  [the longest x1 32 us: per_device(): upstream_all = lax.all_gather(dfinal_low, 'lon', axis=0, tiled=True)]
    unnamed x1 -> x0, blocking collectives: 43.2 us -> none
    pallas_call x0 -> x4, Pallas kernels: none -> 42.2 us  [the longest x1 17.2 us: attn_backward(): pl.pallas_call(functools.partial(attn_bwd_kernel, heads), grid=(items, se...]
    squeeze x24 -> x0, local copies, waits for them, and re-layouts: 31.4 us -> none  [per_device(): (highest, totals), ignored = lax.scan(stats_step, stats_init, blocks_all)]
  transfers between devices with their start and end apart: 19 -> 17, of which waited for: 11 -> 13; matrix products, arithmetic and copies ran while one was open for 26% -> 23% of each run, Pallas kernels for 0% -> 0%
where the time goes in v1:
time: 662 us; the launch traced here: 649 us
  waiting for transfers between devices  336 us (51%)
  matrix products  110 us (17%)
  local copies, waits for them, and re-layouts  94.5 us (14%)
  Pallas kernels  42.2 us (6%)
  other arithmetic  25.6 us (4%)
  starting transfers between devices  24.2 us (4%)
  between operations  15.8 us (2%)
    psum x1, waiting for transfers between devices, per_device(): dpv = lax.psum(lax.psum(dpv.astype(BF16), 'lon'), 'batch')  94.9 us
    dot_general x14, matrix products, contract(): lax.dot_general(left, right, (dims, ((), ())), preferred_element_type=F32)  59.7 us
    psum x2, waiting for transfers between devices, per_device(): vectors = lax.psum(lax.psum(vectors, 'lon'), 'batch')  42 us
    reduce_scatter x1, waiting for transfers between devices, per_device(): lax.psum_scatter(columns_own, 'batch', scatter_dimension=0, tiled=True)  41 us
    dot_general x12, matrix products, product(): return jnp.dot(left, right, preferred_element_type=F32)  40 us
    unnamed x136, local copies, waits for them, and re-layouts  39.5 us
    psum x1, waiting for transfers between devices, per_device(): lax.psum(position_local.astype(BF16), 'batch')  32.7 us
    all_gather x1, waiting for transfers between devices, per_device(): upstream_all = lax.all_gather(dfinal_low, 'lon', axis=0, tiled=True)  32 us
  transfers between devices with their start and end apart: 17, of which 13 were waited for; matrix products, arithmetic and copies ran while one was open for 23% of the time, Pallas kernels for 0%

profile of v1, /device:TPU:14, one launch (start us, length us, event | category | flops | bytes accessed | tf_op | source)
XLA Modules:
  0.0 648.8 jit_solution(16862541365039831635)
XLA Ops:
  28.4 4.5 pool_fwd.1
  36.8 8.8 %copy.159 = bf16[1024,3072]{0,1:T(8,128)(2,1)} copy(bf16[1024,3072]{1,0:T(8,128)(2,1)} %param.41) | data formatting | bytes 12582912 | tf_op args[14]
  50.0 23.9 %all-gather.4.cloned.1.call-done = bf16[2,1024,1024]{2,1,0:T(8,128)(2,1)} async-done(((bf16[2,128,1024]{2,1,0:T(8,128)(2,1)}), bf16[2,1024,1024]{2,1,0:T(8,128)(2,1)}) %all-gather.4.cloned.1.call-update) | async-done | bytes 4194320 | tf_op jit(solution)/shard_map/all_gather | solution.py:275
  74.0 4.8 add_convert_fusion
  80.0 11.7 %attn_fwd.1 = (bf16[2,1024,128]{2,1,0:T(8,128)(2,1)}, f32[2,2,1024]{2,1,0:T(2,128)}) custom-call(bf16[2,1024,128]{2,1,0:T(8,128)(2,1)} %get-tuple-element.190.q_ref, bf16[2,1024,128]{2,1,0:T(8,128)(2,1)} %get-tuple-element.189.k_ref, bf16[2,1024,128]{2,1,0:T(8,128)(2,1)} %get-tuple-element.188.v_ref), custom_call_target="tpu_custom_call" | custom-call | tf_op jit(solution)/shard_map/attn_fwd/pallas_call | solution.py:157
  93.6 5.8 all-to-all-start
  115.2 7.9 %convolution_add_fusion = f32[256,4096]{1,0:T(8,128)} fusion(bf16[256,1024]{1,0:T(8,128)(2,1)} %add_convert_fusion.1, bf16[1024,4096]{1,0:T(8,128)(2,1)} %param.47, f32[4096]{0:T(1024)S(1)} %convert_element_type.226), kind=kOutput, calls=%fused_computation.5 | convolution fusion | flops 2148532224 | bytes 13123584 | tf_op jit(solution)/shard_map/dot_general | solution.py:29
  123.1 7.7 %convert_reduce_fusion = (f32[4096]{0:T(1024)S(1)}, bf16[256,4096]{1,0:T(8,128)(2,1)S(1)}) fusion(f32[256,4096]{1,0:T(8,128)} %convolution_add_fusion, bf16[256,1024]{1,0:T(8,128)(2,1)} %get-tuple-element.183, bf16[4096,1024]{1,0:T(8,128)(2,1)} %param.49), kind=kOutput, calls=%fused_computation.29 | convolution fusion | flops 2169499648 | bytes 15220736 | tf_op jit(solution)/shard_map/dot_general | solution.py:33
  130.8 6.8 %multiply_reduce_fusion = (f32[1024]{0:T(1024)}, f32[256]{0:T(256)S(1)}, f32[256]{0:T(256)S(1)}, f32[1024]{0:T(1024)}, f32[256,1024]{1,0:T(8,128)S(1)}) fusion(f32[256,1024]{1,0:T(8,128)S(1)} %copy-done.13, f32[256]{0:T(256)S(1)} %add_rsqrt_fusion, f32[256]{0:T(256)S(1)} %broadcast_multiply_fusion.5, f32[1024]{0:T(1024)S(1)} %convert_element_type.223, ...), kind=kOutput, calls=%fused_computation.70 | convolution fusion | flops 2149840384 | bytes 12599296 | tf_op jit(solution)/shard_map/dot_general | solution.py:33
  141.7 5.2 all-to-all-start.1
  149.9 4.4 all-to-all-done.1
  156.2 17.2 %attn_bwd.1 = (bf16[2,1024,128]{2,1,0:T(8,128)(2,1)}, bf16[2,1024,128]{2,1,0:T(8,128)(2,1)}, bf16[2,1024,128]{2,1,0:T(8,128)(2,1)}) custom-call(bf16[2,1024,128]{2,1,0:T(8,128)(2,1)} %get-tuple-element.190.q_ref, bf16[2,1024,128]{2,1,0:T(8,128)(2,1)} %get-tuple-element.189.k_ref, bf16[2,1024,128]{2,1,0:T(8,128)(2,1)} %get-tuple-element.188.v_ref, ...), custom_call_target="tpu_custom_call" | custom-call | tf_op jit(solution)/shard_map/attn_bwd/pallas_call | solution.py:211
  179.3 6.6 %all-to-all-start.2 = ((bf16[2,8,128,384]{3,2,0,1:T(8,128)(2,1)}), bf16[2,8,128,384]{3,2,0,1:T(8,128)(2,1)}, u32[]{:S(2)}, u32[]{:S(2)}) async-start(bf16[2,8,128,384]{3,2,0,1:T(8,128)(2,1)} %copy.169), calls=%async_computation.2 | async-start | bytes 3145728 | tf_op jit(solution)/shard_map/all_to_all | solution.py:286
  185.9 8.3 %fusion.31 = bf16[256,1024]{1,0:T(8,128)(2,1)} fusion(f32[256,1024]{1,0:T(8,128)} %copy-done.12, bf16[4096,1024]{1,0:T(8,128)(2,1)} %param.49, f32[256,4096]{1,0:T(8,128)} %convolution_add_fusion, f32[1024]{0:T(1024)S(1)} %convert_element_type.228), kind=kOutput, calls=%fused_computation.53 | convolution fusion | flops 2157707264 | bytes 14159872 | tf_op jit(solution)/shard_map/dot_general | solution.py:29
  211.2 5.5 multiply_reduce_fusion.1
  220.5 8.8 %pool_bwd.1 = (f32[256,256]{1,0:T(8,128)S(1)}, f32[320,1024]{1,0:T(8,128)S(1)}, f32[16,320]{1,0:T(8,128)S(1)}) custom-call(bf16[256,320]{1,0:T(8,128)(2,1)S(1)} %concatenate.40.patches_ref, f32[16,256,64]{2,1,0:T(8,128)S(1)} %copy-done.5, f32[16,320]{1,0:T(8,128)S(1)} %bitcast.206, bf16[320,1024]{1,0:T(8,128)(2,1)S(1)} %copy-done.3, ...), custom_call_target="tpu_custom_call" | custom-call | tf_op jit(solution)/shard_map/pool_bwd/pallas_call | solution.py:129
  230.2 3.9 pad_maximum_fusion
  236.5 12.0 %copy.179 = bf16[1024,4096]{0,1:T(8,128)(2,1)} copy(bf16[1024,4096]{1,0:T(8,128)(2,1)} %param.47) | data formatting | bytes 16777216 | tf_op args[20]
  251.0 30.2 %all-reduce.9.cloned.1.call-done = f32[19648]{0:T(1024)} async-done(((f32[19648]{0:T(1024)}), f32[19648]{0:T(1024)}) %all-reduce.9.cloned.1.call-update) | async-done | bytes 78608 | tf_op jit(solution)/shard_map/psum | solution.py:378
  284.4 94.9 %all-reduce.13.cloned.1.call-done = (bf16[320,1024]{1,0:T(8,128)(2,1)}, bf16[4,8,32,2240]{3,2,1,0:T(8,128)(2,1)}) async-done(((bf16[320,1024]{1,0:T(8,128)(2,1)}, bf16[4,8,32,2240]{3,2,1,0:T(8,128)(2,1)}), (bf16[320,1024]{1,0:T(8,128)(2,1)}, bf16[4,8,32,2240]{3,2,1,0:T(8,128)(2,1)})) %all-reduce.13.cloned.1.call-update) | async-done | bytes 5242896 | tf_op jit(solution)/shard_map/psum | solution.py:379
  380.0 5.0 bitcast_convert_fusion
  387.7 30.3 %all-gather.6.cloned.1.call-done = bf16[2048,1024]{1,0:T(8,128)(2,1)} async-done(((bf16[256,1024]{1,0:T(8,128)(2,1)}), bf16[2048,1024]{1,0:T(8,128)(2,1)}) %all-gather.6.cloned.1.call-update) | async-done | bytes 4194320 | tf_op jit(solution)/shard_map/all_gather | solution.py:298
  418.0 6.6 %fusion.128 = f32[2048,512]{1,0:T(8,128)} fusion(bf16[2048,1024]{1,0:T(8,128)(2,1)} %all-gather.6.cloned.1.call-done, bf16[1024,512]{0,1:T(8,128)(2,1)S(1)} %bitcast.237), kind=kOutput, calls=%fused_computation.242 | convolution fusion | flops 2147483648 | bytes 9437184 | tf_op jit(solution)/shard_map/dot_general | solution.py:29
  424.6 32.0 %all-gather.8.cloned.1.call-done = bf16[2048,1024]{1,0:T(8,128)(2,1)} async-done(((bf16[256,1024]{1,0:T(8,128)(2,1)}), bf16[2048,1024]{1,0:T(8,128)(2,1)}) %all-gather.8.cloned.1.call-update) | async-done | bytes 4194320 | tf_op jit(solution)/shard_map/all_gather | solution.py:319
  456.6 12.7 %convolution_convert_fusion.2 = bf16[1024,512]{0,1:T(8,128)(2,1)} fusion(bf16[2048,1024]{1,0:T(8,128)(2,1)} %all-gather.6.cloned.1.call-done, f32[2048,512]{1,0:T(8,128)} %fusion.128, bf16[2048,1024]{1,0:T(8,128)(2,1)} %all-gather.8.cloned.1.call-done, bf16[512,1024]{1,0:T(8,128)(2,1)S(1)} %bitcast.238, f32[512]{0:T(512)S(1)} %bitcast.253), kind=kOutput, calls=%fused_computation.44 | convolution fusion | flops 4316463104 | bytes 14682112 | tf_op jit(solution)/shard_map/dot_general | solution.py:33
  482.3 11.8 %all-reduce.11.cloned.1.call-done = f32[19648]{0:T(1024)} async-done(((f32[19648]{0:T(1024)}), f32[19648]{0:T(1024)}) %all-reduce.11.cloned.1.call-update) | async-done | bytes 78608 | tf_op jit(solution)/shard_map/psum | solution.py:378
  497.2 7.1 %fusion.26 = bf16[512,1024]{1,0:T(8,128)(2,1)} fusion(bf16[2048,1024]{1,0:T(8,128)(2,1)} %all-gather.8.cloned.1.call-done, f32[2048,512]{1,0:T(8,128)} %fusion.128, f32[512]{0:T(512)S(1)} %bitcast.254), kind=kOutput, calls=%fused_computation.43 | convolution fusion | flops 2158493696 | bytes 9439232 | tf_op jit(solution)/shard_map/dot_general | solution.py:33
  512.1 32.7 %all-reduce.15.cloned.1.call-done = (bf16[4,32,1024]{2,1,0:T(8,128)(2,1)}, bf16[320,1024]{1,0:T(8,128)(2,1)}) async-done(((bf16[4,32,1024]{2,1,0:T(8,128)(2,1)}, bf16[320,1024]{1,0:T(8,128)(2,1)}), (bf16[4,32,1024]{2,1,0:T(8,128)(2,1)}, bf16[320,1024]{1,0:T(8,128)(2,1)})) %all-reduce.15.cloned.1.call-update) | async-done | bytes 917520 | tf_op jit(solution)/shard_map/psum | solution.py:359
  552.3 13.6 %reduce-scatter.5.cloned.1.call-done = bf16[1,1,32,2240]{3,2,1,0:T(8,128)(2,1)} async-done(((bf16[4,1,32,2240]{3,2,1,0:T(8,128)(2,1)}), bf16[1,1,32,2240]{3,2,1,0:T(8,128)(2,1)}) %reduce-scatter.5.cloned.1.call-update) | async-done | bytes 143376 | tf_op jit(solution)/shard_map/reduce_scatter | solution.py:370
  566.8 41.0 %reduce-scatter.7.cloned.1.call-done = bf16[256,896]{0,1:T(8,128)(2,1)} async-done(((bf16[1024,896]{0,1:T(8,128)(2,1)}), bf16[256,896]{0,1:T(8,128)(2,1)}) %reduce-scatter.7.cloned.1.call-update) | async-done | bytes 458768 | tf_op jit(solution)/shard_map/reduce_scatter | solution.py:347
  609.8 4.2 all-to-all-start.3
  616.4 18.6 %reduce-scatter.9.cloned.1.call-done = bf16[128,1024]{1,0:T(8,128)(2,1)} async-done(((bf16[512,1024]{1,0:T(8,128)(2,1)}), bf16[128,1024]{1,0:T(8,128)(2,1)}) %reduce-scatter.9.cloned.1.call-update) | async-done | bytes 262160 | tf_op jit(solution)/shard_map/reduce_scatter | solution.py:340
  (318 shorter events, 138.4 us)
Async XLA Ops:
  7.2 27.3 %copy-start = (bf16[1024,1024]{1,0:T(8,128)(2,1)S(1)}, bf16[1024,1024]{1,0:T(8,128)(2,1)}, u32[]{:S(2)}) copy-start(bf16[1024,1024]{1,0:T(8,128)(2,1)} %param.37) | copy-start | bytes 6291460
  7.2 66.7 %all-gather.4.cloned.1.call-start = ((), (), s32[]{:S(2)}) async-start(), calls=%async_computation.7 | async-start | bytes 4718592 | tf_op jit(solution)/shard_map/all_gather | solution.py:275
  8.6 11.6 %collective-permute-start = (bf16[2,2,48,1,64]{4,2,3,1,0:T(8,128)(2,1)S(1)}, bf16[2,2,48,1,64]{4,2,3,1,0:T(8,128)(2,1)S(1)}, u32[]{:S(2)}, u32[]{:S(2)}) collective-permute-start(bf16[2,2,48,1,64]{4,2,3,1,0:T(8,128)(2,1)S(1)} %pad_maximum_fusion.5), channel_id=1, source_target_pairs={{0,1},{1,2},{2,3},{3,4},{4,5},{5,6},{6,7},{7,0},{8,9},{9,10},{10,1... | collective-permute-start | bytes 73736 | tf_op jit(solution)/shard_map/ppermute | solution.py:241
  78.7 20.6 %copy-start.38 = (s32[64]{0:T(128)S(1)}, s32[64]{0:T(128)}, u32[]{:S(2)}) copy-start(s32[64]{0:T(128)} %copy-done.37) | copy-start | bytes 772
  93.6 15.0 %all-to-all-start = ((bf16[2,8,128,128]{3,2,0,1:T(8,128)(2,1)}), bf16[2,8,128,128]{3,2,0,1:T(8,128)(2,1)}, u32[]{:S(2)}, u32[]{:S(2)}) async-start(bf16[2,8,128,128]{3,2,0,1:T(8,128)(2,1)} %copy.160), calls=%async_computation | async-start | bytes 1048576 | tf_op jit(solution)/shard_map/all_to_all | solution.py:286
  114.1 16.7 %copy-start.34 = (f32[256]{0:T(256)}, f32[256]{0:T(256)S(1)}, u32[]{:S(2)}) copy-start(f32[256]{0:T(256)S(1)} %add_rsqrt_fusion) | copy-start | bytes 3076
  141.7 12.6 %all-to-all-start.1 = ((bf16[2,8,128,128]{3,2,0,1:T(8,128)(2,1)}), bf16[2,8,128,128]{3,2,0,1:T(8,128)(2,1)}, u32[]{:S(2)}, u32[]{:S(2)}) async-start(bf16[2,8,128,128]{3,2,0,1:T(8,128)(2,1)} %bitcast.226), calls=%async_computation.1 | async-start | bytes 1048576 | tf_op jit(solution)/shard_map/all_to_all | solution.py:291
  179.3 25.4 %all-to-all-start.2 = ((bf16[2,8,128,384]{3,2,0,1:T(8,128)(2,1)}), bf16[2,8,128,384]{3,2,0,1:T(8,128)(2,1)}, u32[]{:S(2)}, u32[]{:S(2)}) async-start(bf16[2,8,128,384]{3,2,0,1:T(8,128)(2,1)} %copy.169), calls=%async_computation.2 | async-start | bytes 3145728 | tf_op jit(solution)/shard_map/all_to_all | solution.py:286
  185.9 95.3 %all-reduce.9.cloned.1.call-start = ((), (), s32[]{:S(2)}) async-start(), calls=%async_computation.8 | async-start | bytes 163840 | tf_op jit(solution)/shard_map/psum | solution.py:378
  218.0 12.2 %copy-start.25 = (bf16[4,8,32,192]{3,2,1,0:T(8,128)(2,1)S(1)}, bf16[4,8,32,192]{3,2,1,0:T(8,128)(2,1)}, u32[]{:S(2)}) copy-start(bf16[4,8,32,192]{3,2,1,0:T(8,128)(2,1)} %convolution_convert_fusion.5) | copy-start | bytes 1179652
  230.2 149.2 %all-reduce.13.cloned.1.call-start = ((), (), s32[]{:S(2)}) async-start(), calls=%async_computation.15 | async-start | bytes 10747904 | tf_op jit(solution)/shard_map/psum | solution.py:379
  235.1 182.9 %all-gather.6.cloned.1.call-start = ((), (), s32[]{:S(2)}) async-start(), calls=%async_computation.11 | async-start | bytes 4718592 | tf_op jit(solution)/shard_map/all_gather | solution.py:298
  235.7 221.0 %all-gather.8.cloned.1.call-start = ((), (), s32[]{:S(2)}) async-start(), calls=%async_computation.12 | async-start | bytes 4718592 | tf_op jit(solution)/shard_map/all_gather | solution.py:319
  236.3 257.8 %all-reduce.11.cloned.1.call-start = ((), (), s32[]{:S(2)}) async-start(), calls=%async_computation.9 | async-start | bytes 163840 | tf_op jit(solution)/shard_map/psum | solution.py:378
  248.5 35.1 %copy-start.11 = (f32[256,1024]{1,0:T(8,128)S(1)}, f32[256,1024]{1,0:T(8,128)}, u32[]{:S(2)}) copy-start(f32[256,1024]{1,0:T(8,128)} %copy-done.10) | copy-start | bytes 3145732
  248.5 130.9 %copy-start.60 = (u32[32]{0:T(128)S(1)}, u32[32]{0:T(128)}, u32[]{:S(2)}) copy-start(u32[32]{0:T(128)} %constant.173) | copy-start | bytes 388
  248.5 131.5 %copy-start.24 = (bf16[2,1024,384]{2,1,0:T(8,128)(2,1)S(1)}, bf16[2,1024,384]{2,1,0:T(8,128)(2,1)}, u32[]{:S(2)}) copy-start(bf16[2,1024,384]{2,1,0:T(8,128)(2,1)} %copy-done.23) | copy-start | bytes 4718596
  281.3 263.5 %all-reduce.15.cloned.1.call-start = ((), (), s32[]{:S(2)}) async-start(), calls=%async_computation.16 | async-start | bytes 1835008 | tf_op jit(solution)/shard_map/psum | solution.py:359
  379.4 186.5 %reduce-scatter.5.cloned.1.call-start = ((), (), s32[]{:S(2)}) async-start(), calls=%async_computation.10 | async-start | bytes 737280 | tf_op jit(solution)/shard_map/reduce_scatter | solution.py:370
  380.0 38.0 %copy-start.29 = (bf16[1024,4,1,128]{0,3,2,1:T(8,128)(2,1)S(1)}, bf16[1024,4,1,128]{0,3,2,1:T(8,128)(2,1)}, u32[]{:S(2)}) copy-start(bf16[1024,4,1,128]{0,3,2,1:T(8,128)(2,1)} %constant_dynamic-slice_fusion.1) | copy-start | bytes 3145732
  387.6 220.2 %reduce-scatter.7.cloned.1.call-start = ((), (), s32[]{:S(2)}) async-start(), calls=%async_computation.13 | async-start | bytes 2293760 | tf_op jit(solution)/shard_map/reduce_scatter | solution.py:347
  418.0 38.6 %copy-start.30 = (bf16[4,1,128,1024]{3,2,1,0:T(8,128)(2,1)S(1)}, bf16[4,1,128,1024]{3,2,1,0:T(8,128)(2,1)}, u32[]{:S(2)}) copy-start(bf16[4,1,128,1024]{3,2,1,0:T(8,128)(2,1)} %constant_dynamic-slice_fusion.2) | copy-start | bytes 3145732
  472.5 162.6 %reduce-scatter.9.cloned.1.call-start = ((), (), s32[]{:S(2)}) async-start(), calls=%async_computation.14 | async-start | bytes 1310720 | tf_op jit(solution)/shard_map/reduce_scatter | solution.py:340
  476.1 18.9 %copy-start.22 = (bf16[1024,320]{0,1:T(8,128)(2,1)S(1)}, bf16[1024,320]{0,1:T(8,128)(2,1)}, u32[]{:S(2)}) copy-start(bf16[1024,320]{0,1:T(8,128)(2,1)} %copy-done.21) | copy-start | bytes 1966084
  476.5 3.2 collective-permute-start.1
  479.3 2.1 collective-permute-start.2
  497.2 13.8 %slice-start.1 = ((f32[19648]{0:T(1024)}), f32[2048]{0:T(1024)S(1)}, s32[]{:S(2)}) async-start(f32[19648]{0:T(1024)} %all-reduce.11.cloned.1.call-done), calls=%async_computation.18 | async-start | bytes 16384 | tf_op jit(solution)/shard_map/slice | solution.py:386
  497.2 14.3 %slice-start.2 = ((f32[19648]{0:T(1024)}), f32[4096]{0:T(1024)S(1)}, s32[]{:S(2)}) async-start(f32[19648]{0:T(1024)} %all-reduce.11.cloned.1.call-done), calls=%async_computation.19 | async-start | bytes 32768 | tf_op jit(solution)/shard_map/slice | solution.py:387
  504.3 44.8 %copy-start.57 = (s32[240]{0:T(256)S(1)}, s32[240]{0:T(256)}, u32[]{:S(2)}) copy-start(s32[240]{0:T(256)} %copy-done.56) | copy-start | bytes 2884
  549.5 90.4 %copy-start.36 = (f32[32,240]{1,0:T(8,128)}, f32[32,240]{1,0:T(8,128)S(1)}, u32[]{:S(2)}) copy-start(f32[32,240]{1,0:T(8,128)S(1)} %fusion.45) | copy-start | bytes 92164
  609.8 27.1 %all-to-all-start.3 = ((bf16[8,32,896]{2,1,0:T(8,128)(2,1)}), bf16[8,32,896]{2,1,0:T(8,128)(2,1)S(1)}, u32[]{:S(2)}, u32[]{:S(2)}) async-start(bf16[8,32,896]{2,1,0:T(8,128)(2,1)} %bitcast.74), calls=%async_computation.5 | async-start | bytes 917504 | tf_op jit(solution)/shard_map/all_to_all | solution.py:348
  614.0 27.5 %copy-start.1 = (bf16[1024,1024]{1,0:T(8,128)(2,1)S(1)}, bf16[1024,1024]{1,0:T(8,128)(2,1)}, u32[]{:S(2)}) copy-start(bf16[1024,1024]{1,0:T(8,128)(2,1)} %param.37) | copy-start | bytes 6291460
  (49 other events, 259.1 us)
Sparse Core Ops, SparseCore 0:
  36.8 37.1 all-gather.3
  230.3 50.8 all-reduce.8
  285.0 94.3 all-reduce.12
  381.3 36.6 all-gather.5
  419.9 36.7 all-gather.7
  458.9 35.1 all-reduce.10
  497.1 47.6 all-reduce.14
  547.1 18.7 reduce-scatter.4
  568.2 39.5 reduce-scatter.6
  609.9 25.0 reduce-scatter.8
